TPU v7x, 256 devices: a whole 4x4x8 slice. The times are simulated.
256 devices in a mesh: band: 8 (over y, core), chan: 32 (over z, x).
Axes of the slice: x: 4, y: 4, z: 8, core: 2. Of those that a mesh axis runs over, the one named last changes fastest.
Arguments:
- spectra: bfloat16 [2, 1024, 512, 256], P(None, 'band', None, 'chan'), may hold values from -6 to 6
- exponents: int32 [1024, 512], P('band'), may hold values from -2 to 2
- counts: int32 [512], P('chan'), may hold values from 128 to 256
Outputs:
- visibilities: bfloat16 [512, 2, 1024, 1024], P('chan', None, 'band')
All inputs are finite; a program needn't handle non-finite values.
Results may differ from a plain program's by a relative error of at most 0.004.
Values may be sent and summed in bfloat16 or wider, within the bound.
A program may use at most 128 MiB of HBM per device.

v0:
```python
import jax
import jax.numpy as jnp
from jax import lax
from jax.sharding import PartitionSpec as P

BLOCK = 64


def power_scale(exponents):
    scale = jnp.zeros(exponents.shape, jnp.float32)
    for power in range(-2, 3):
        scale = scale + jnp.where(exponents == power, jnp.float32(2.0**power), jnp.float32(0.0))
    return scale


def gram_tile(row_form, piece):
    product = jnp.einsum("crt,cjt->crj", row_form, piece, preferred_element_type=jnp.float32)
    return product.reshape(product.shape[0], 2, product.shape[1] // 2, product.shape[2])


def lower_mask(row_start, rows, cols):
    row_block = (row_start + jnp.arange(rows, dtype=jnp.int32)) // BLOCK
    col_block = jnp.arange(cols, dtype=jnp.int32) // BLOCK
    return (row_block[:, None] >= col_block[None, :]).astype(jnp.float32)


def forms(turned, own_counts):
    samples = turned.shape[3]
    live = jnp.arange(samples, dtype=jnp.int32)[None, :] < own_counts[:, None]
    turned = jnp.where(live[None, None], turned, jnp.zeros((), jnp.bfloat16))
    plain = jnp.transpose(jnp.concatenate([turned[0], turned[1]], axis=-1), (1, 0, 2))
    rotated = jnp.transpose(jnp.concatenate([turned[1], -turned[0]], axis=-1), (1, 0, 2))
    return (plain, jnp.concatenate([plain, rotated], axis=1))


def local(spectra, exponents, counts):
    scale = power_scale(exponents)
    scaled = (spectra.astype(jnp.float32) * scale[None, :, :, None]).astype(jnp.bfloat16)
    turned = lax.all_to_all(scaled, "chan", split_axis=2, concat_axis=3, tiled=True)
    band_rows = turned.shape[1]
    plain, row_form = forms(turned, counts)
    channels = plain.shape[0]
    own_band = lax.axis_index("band")
    row_start = own_band * band_rows
    piece = lax.all_gather(plain, "band", axis=1, tiled=True)
    count = piece.shape[1]

    def compute():
        return gram_tile(row_form, piece) * lower_mask(row_start, band_rows, count)

    def nothing():
        return jnp.zeros((channels, 2, band_rows, count), jnp.float32)

    tile = lax.cond(jnp.int32(0) < row_start + band_rows, compute, nothing)
    return (tile / counts.astype(jnp.float32)[:, None, None, None]).astype(jnp.bfloat16)


def solution(mesh):
    placed = (P(None, "band", None, "chan"), P("band", None), P("chan"))
    return jax.shard_map(
        local, mesh=mesh, in_specs=placed, out_specs=P("chan", None, "band", None), check_vma=False
    )
```

profile of v0, /device:TPU:25, one launch (start us, length us, event | category | flops | bytes accessed | tf_op | source)
XLA Modules:
  0.0 213.0 jit_solution(9018452588870682759)
XLA Ops:
  6.5 0.0 copy-start
  6.5 3.9 %copy.10 = bf16[2,128,512,8]{1,3,0,2:T(8,128)(2,1)S(1)} copy(bf16[2,128,512,8]{2,3,1,0:T(8,128)(2,1)} %param.5) | data formatting | bytes 4194304 | tf_op args[0]
  10.4 0.0 copy-done
  10.4 0.1 select_add_fusion
  10.6 0.1 copy.11
  10.7 0.0 copy-start.1
  10.7 1.8 multiply_convert_fusion
  12.5 11.0 %all-to-all-start = ((bf16[2,128,512,8]{1,3,0,2:T(8,128)(2,1)}), bf16[2,128,512,8]{1,3,0,2:T(8,128)(2,1)S(1)}, u32[]{:S(2)}, u32[]{:S(2)}) async-start(bf16[2,128,512,8]{1,3,0,2:T(8,128)(2,1)} %multiply_convert_fusion), calls=%async_computation | async-start | bytes 4194304 | tf_op jit(solution)/shard_map/all_to_all | solution.py:39
  23.5 0.0 all-gather.2.cloned.1.call-start
  23.6 0.0 copy-done.1
  23.6 0.1 iota_compare_fusion
  23.7 48.3 %all-to-all-done = bf16[2,128,512,8]{1,3,0,2:T(8,128)(2,1)S(1)} async-done(((bf16[2,128,512,8]{1,3,0,2:T(8,128)(2,1)}), bf16[2,128,512,8]{1,3,0,2:T(8,128)(2,1)S(1)}, u32[]{:S(2)}, u32[]{:S(2)}) %all-to-all-start) | async-done | bytes 2097184 | tf_op jit(solution)/shard_map/all_to_all | solution.py:39
  72.0 0.8 bitcast_select_fusion
  72.8 0.2 slice_bitcast_fusion.1
  73.1 0.1 fusion.3
  73.2 1.6 maximum_bitcast_fusion
  74.8 0.0 all-gather.2.cloned.1.call-update
  74.9 4.2 %pad_maximum_fusion = bf16[16,256,512]{1,2,0:T(8,128)(2,1)} fusion(bf16[16,128,512]{1,2,0:T(8,128)(2,1)S(1)} %get-tuple-element.26, bf16[16,128,512]{1,2,0:T(8,128)(2,1)} %get-tuple-element.25), kind=kLoop, calls=%fused_computation.14 | loop fusion | flops 8388608 | bytes 8388608 | tf_op jit(solution)/shard_map/concatenate | solution.py:33
  79.1 87.7 %all-gather.2.cloned.1.call-done = bf16[16,1024,512]{1,2,0:T(8,128)(2,1)} async-done(((bf16[16,128,512]{1,2,0:T(8,128)(2,1)}), bf16[16,1024,512]{1,2,0:T(8,128)(2,1)}) %all-gather.2.cloned.1.call-update) | async-done | bytes 16777232 | tf_op jit(solution)/shard_map/all_gather | solution.py:45
  166.7 29.7 %conditional.1 = (f32[16,2,128,1024]{3,2,1,0:T(8,128)}) conditional(s32[]{:T(128)} %convert_element_type.22, () %tuple.11, (bf16[16,256,512]{1,2,0:T(8,128)(2,1)}, bf16[16,1024,512]{1,2,0:T(8,128)(2,1)}, s32[]{:T(128)}) %tuple.12), branch_computations={%region_0.1_spmd, %region_1.2_spmd} | conditional | flops 4299433984 | bytes 72360968 | solution.py:54
  166.7 17.3 %fusion.4 = f32[16,256,1024]{2,1,0:T(8,128)} fusion(bf16[16,256,512]{1,2,0:T(8,128)(2,1)} %get-tuple-element.20, bf16[16,1024,512]{1,2,0:T(8,128)(2,1)} %get-tuple-element.21), kind=kOutput, calls=%fused_computation.24 | convolution fusion | flops 4294967296 | bytes 37748736 | tf_op jit(solution)/shard_map/cond/branch_1_fun/crt,cjt->crj/dot_general | solution.py:17
  184.1 0.1 compare_convert_fusion
  184.2 12.2 %broadcast_multiply_fusion = f32[16,2,128,1024]{3,2,1,0:T(8,128)} fusion(f32[16,2,128,1024]{3,2,1,0:T(8,128)} %bitcast.18, f32[128,1024]{1,0:T(8,128)S(1)} %compare_convert_fusion), kind=kLoop, calls=%fused_computation | loop fusion | flops 4194304 | bytes 34078720 | tf_op jit(solution)/shard_map/cond/branch_1_fun/mul | solution.py:49
  196.4 9.7 %divide_convert_fusion = bf16[16,2,128,1024]{3,2,1,0:T(8,128)(2,1)} fusion(f32[16,2,128,1024]{3,2,1,0:T(8,128)} %get-tuple-element.27, f32[16]{0:T(128)S(1)} %convert_element_type.25), kind=kLoop, calls=%fused_computation.13 | loop fusion | flops 8388608 | bytes 25165888 | tf_op jit(solution)/shard_map/convert_element_type | solution.py:55
  (3 shorter events, 0.0 us)
Async XLA Ops:
  6.5 3.9 %copy-start = (s32[128,512]{1,0:T(8,128)S(1)}, s32[128,512]{1,0:T(8,128)}, u32[]{:S(2)}) copy-start(s32[128,512]{1,0:T(8,128)} %param.6) | copy-start | bytes 786436
  10.7 12.9 %copy-start.1 = (s32[16]{0:T(128)S(1)}, s32[16]{0:T(128)}, u32[]{:S(2)}) copy-start(s32[16]{0:T(128)} %param.7) | copy-start | bytes 196
  12.5 59.5 %all-to-all-start = ((bf16[2,128,512,8]{1,3,0,2:T(8,128)(2,1)}), bf16[2,128,512,8]{1,3,0,2:T(8,128)(2,1)S(1)}, u32[]{:S(2)}, u32[]{:S(2)}) async-start(bf16[2,128,512,8]{1,3,0,2:T(8,128)(2,1)} %multiply_convert_fusion), calls=%async_computation | async-start | bytes 4194304 | tf_op jit(solution)/shard_map/all_to_all | solution.py:39
  23.5 143.2 %all-gather.2.cloned.1.call-start = ((), (), s32[]{:S(2)}) async-start(), calls=%async_computation.1 | async-start | bytes 18874368 | tf_op jit(solution)/shard_map/all_gather | solution.py:45
Sparse Core Ops, SparseCore 0:
  75.0 91.7 all-gather.1
where the time goes:
time: 215 us; the launch traced here: 213 us
  waiting for transfers between devices  136 us (63%)
  other arithmetic  30.8 us (14%)
  matrix products  17.3 us (8%)
  between operations  13.5 us (6%)
  starting transfers between devices  11.1 us (5%)
  local copies, waits for them, and re-layouts  4.23 us (2%)
    all_gather x1, waiting for transfers between devices, local(): piece = lax.all_gather(plain, 'band', axis=1, tiled=True)  87.7 us
    all_to_all x1, waiting for transfers between devices, local(): lax.all_to_all(scaled, 'chan', split_axis=2, concat_axis=3, tiled=True)  48.3 us
    dot_general x1, matrix products, gram_tile(): jnp.einsum('crt,cjt->crj', row_form, piece, preferred_element_type=jnp.fl...  17.3 us
    mul x1, other arithmetic, compute(): return gram_tile(row_form, piece) * lower_mask(row_start, band_rows, count)  12.2 us
    all_to_all x1, starting transfers between devices, local(): lax.all_to_all(scaled, 'chan', split_axis=2, concat_axis=3, tiled=True)  11 us
    convert_element_type x1, other arithmetic, local(): (tile / counts.astype(jnp.float32)[:, None, None, None]).astype(jnp.bfloa...  9.72 us
  transfers between devices with their start and end apart: 2, of which 2 were waited for; matrix products, arithmetic and copies ran while one was open for 2% of the time, Pallas kernels for 0%

commit v1 on v0

v1 whole, which is shorter than its diff:
```python
import jax
import jax.numpy as jnp
from jax import lax
from jax.experimental import pallas as pl
from jax.experimental.pallas import tpu as pltpu
from jax.sharding import PartitionSpec as P

MESH = pl.DeviceIdType.MESH
BLOCK = 64
BANDS, CORES, YS = 8, 2, 4
ZS, XS = 8, 4
CHANS = ZS * XS
ROWS = 128
OWN = 16
SAMPLES = 8
UNIT = 2 * SAMPLES
DEPTH = CHANS * UNIT
WIDE = 2 * ROWS
GROUPS = 4
GROUP = OWN // GROUPS
EARLY = OWN - GROUP
CHUNK = 4
PARTS = CHANS // CHUNK
STEPS = GROUPS * PARTS
WHOLE = (7, 13, 20, 26)
AHEAD = 12
BY_ONE = 24
LANES = 128
SPANS = CHANS * OWN // LANES
LAG = 3
FIRST = 4
FEW = 28
FLIGHT = 4
OUT_PARTS = 6


def power_scale(exponents):
    scale = jnp.zeros(exponents.shape, jnp.float32)
    for power in range(-2, 3):
        scale = scale + jnp.where(exponents == power, jnp.float32(2.0**power), jnp.float32(0.0))
    return scale


def mod(a, n):
    return a % n if isinstance(a, int) else lax.rem(a, jnp.full_like(a, n))


def div(a, n):
    return a // n if isinstance(a, int) else lax.div(a, jnp.full_like(a, n))


def flip(a, b, bits):
    return sum(mod(div(a, 1 << n) + div(b, 1 << n), 2) * (1 << n) for n in range(bits))


def offset(k):
    return 2 * div(k, 2 * CHUNK) + mod(k, 2), div(mod(k, CHUNK), 2) + 2 * mod(div(k, CHUNK), 2)


def source(chan, k):
    dz, dx = offset(k)
    return flip(div(chan, XS), dz, 3) * XS + mod(mod(chan, XS) + dx, XS)


def target(chan, k):
    dz, dx = offset(k)
    return flip(div(chan, XS), dz, 3) * XS + mod(mod(chan, XS) + XS - dx, XS)


def lower(tile, first):
    line = lax.broadcasted_iota(jnp.int32, tile.shape, 0)
    column = lax.broadcasted_iota(jnp.int32, tile.shape, 1)
    limit = jnp.where(line < BLOCK, BLOCK, 2 * BLOCK) + first
    return jnp.where(column < limit, tile, 0.0)


def kernel(
    counts_hbm, exponents_ref, x_ref, out_ref, buf, forms, shares, counts_ref, times, powers, raw, wide, narrow, xs, load_sem,
    a2a_recv, left_recv, right_recv, relay_recv, core_recv, a2a_send, y_send, own_send, relay_send, core_send,
):
    band = lax.axis_index("band")
    chan = lax.axis_index("chan")
    y, core = div(band, CORES), mod(band, CORES)
    partner = band + 1 - 2 * core
    up, down, far = mod(y + 1, YS), mod(y + YS - 1, YS), mod(y + 2, YS)
    slow = (y == 2).astype(jnp.int32)
    relay = 9 + 3 * slow
    due_far = 14 + 3 * slow, 21 + 2 * slow, 27 + 2 * slow
    up_band, down_band, far_band = up * CORES + core, down * CORES + core, far * CORES + core

    barrier = pltpu.get_barrier_semaphore()

    def greet(k, carry):
        pl.semaphore_signal(barrier, inc=1, device_id=(band, target(chan, k)), device_id_type=MESH)
        return carry

    def drain(ref, sem):
        pltpu.make_async_copy(ref, ref, sem).wait()

    def span(n):
        return flip(div(chan, 2 * XS), n, 2)

    def lanes(n):
        return pl.ds(pl.multiple_of(span(n) * LANES, LANES), LANES)

    loads = [
        pltpu.make_async_copy(exponents_ref, powers, load_sem.at[SPANS]),
        pltpu.make_async_copy(counts_hbm, counts_ref, load_sem.at[SPANS + 1]),
    ] + [pltpu.make_async_copy(x_ref.at[:, :, lanes(n)], raw.at[n], load_sem.at[n]) for n in range(SPANS)]
    for load in loads:
        load.start()

    for other in (up_band, down_band, partner):
        pl.semaphore_signal(barrier, inc=1, device_id=(other, chan), device_id_type=MESH)
    lax.fori_loop(1, CHANS, greet, 0)

    def turn(n):
        drain(raw.at[n], load_sem.at[n])
        scale = power_scale(powers[:, lanes(n)])
        for part in range(2):
            wide[part] = raw[n, part].astype(jnp.float32)
            for t in range(SAMPLES):
                tile = wide[part, pl.ds(t, ROWS, stride=SAMPLES), :] * scale
                narrow[pl.ds(part * SAMPLES + t, LANES, stride=UNIT), :] = tile.T

        def pack(d, carry):
            own = narrow[pl.ds(pl.multiple_of(d * (OWN * UNIT), OWN * UNIT), OWN * UNIT), :]
            xs[span(n) * (LANES // OWN) + d] = own.astype(jnp.bfloat16).reshape(GROUPS, GROUP, UNIT, ROWS)
            return carry

        lax.fori_loop(0, LANES // OWN, pack, 0)

    loads[0].wait()
    turn(0)
    for g in range(GROUPS):
        pltpu.make_async_copy(xs.at[chan, g], buf.at[band, g, 0], a2a_recv.at[g * PARTS]).start()

    pl.semaphore_wait(barrier, CHANS + 2)

    def scatter(s):
        g, part = div(s, PARTS), mod(s, PARTS)

        for n in range(CHUNK):
            k = part * CHUNK + n
            to = target(chan, k)

            @pl.when(k > 0)
            def _():
                pltpu.make_async_remote_copy(
                    src_ref=xs.at[to, g], dst_ref=buf.at[band, g, k],
                    send_sem=a2a_send, recv_sem=a2a_recv.at[s],
                    device_id=(band, to), device_id_type=MESH,
                ).start()

    def scatter_all(first, end):
        def one(s, carry):
            scatter(s)
            return carry

        lax.fori_loop(first, end, one, 0)

    scatter_all(0, 2)
    turn(1)
    scatter_all(2, 4)

    piece = lax.broadcasted_iota(jnp.int32, times.shape, 0)
    row = lax.broadcasted_iota(jnp.int32, times.shape, 1)
    times[...] = source(chan, piece) * SAMPLES + mod(row, SAMPLES)
    loads[1].wait()
    for c in range(GROUP):
        shares[c] = 1.0 / jnp.full(shares.shape[1:], counts_ref[EARLY + c], jnp.int32).astype(jnp.float32)

    def chunk(of_band, s):
        g, part = div(s, PARTS), mod(s, PARTS)
        return buf.at[of_band, g, pl.ds(part * CHUNK, CHUNK)]

    def send(of_band, s, to_band, send_sem, recv_sem):
        ref = chunk(of_band, s)
        pltpu.make_async_remote_copy(
            src_ref=ref, dst_ref=ref, send_sem=send_sem, recv_sem=recv_sem,
            device_id=(to_band, chan), device_id_type=MESH,
        ).start()

    def prepare(g, c):
        slot = mod(g, 2)
        own = buf[band, g, :, c].astype(jnp.float32)
        own = jnp.where(times[...] < counts_ref[g * GROUP + c], own, 0.0)
        swapped = jnp.concatenate([own[:, SAMPLES:], -own[:, :SAMPLES]], axis=1)
        forms[slot, c, :ROWS] = own.astype(jnp.bfloat16).reshape(DEPTH, ROWS).T
        forms[slot, c, ROWS:] = swapped.astype(jnp.bfloat16).reshape(DEPTH, ROWS).T

    def gram(g, q, diagonal):
        slot = mod(g, 2)
        columns = pl.ds(pl.multiple_of(q * WIDE, WIDE), WIDE)

        for c in range(GROUP):
            right = jnp.concatenate(
                [buf[2 * q, g, :, c].reshape(DEPTH, ROWS), buf[2 * q + 1, g, :, c].reshape(DEPTH, ROWS)], axis=1
            )
            share = 1.0 / jnp.full((1, WIDE), counts_ref[g * GROUP + c], jnp.int32).astype(jnp.float32)
            product = jnp.dot(forms[slot, c], right, preferred_element_type=jnp.float32) * share
            for part in range(2):
                tile = product[part * ROWS : (part + 1) * ROWS]
                if diagonal:
                    tile = lower(tile, core * ROWS)
                out_ref[g * GROUP + c, part, :, columns] = tile.astype(jnp.bfloat16)

    def front(s, carry):
        @pl.when(s < STEPS)
        def _():
            drain(chunk(band, s), a2a_recv.at[s])

            @pl.when(y < 2)
            def _():
                send(band, s, up_band, y_send.at[0], left_recv.at[s])

            @pl.when((y == 1) & (mod(s, 2) == 1))
            def _():
                send(band, s, down_band, y_send.at[1], right_recv.at[s])

            @pl.when(core == 0)
            def _():
                send(band, s, partner, core_send.at[0], core_recv.at[0, div(s, PARTS)])

        @pl.when((s > 2) & (s < AHEAD - FIRST))
        def _():
            scatter(2 * s + FIRST)
            scatter(2 * s + FIRST + 1)

        @pl.when((s >= AHEAD - FIRST) & (s + AHEAD < STEPS))
        def _():
            scatter(s + AHEAD)

        return carry

    def pass_on(j, carry):
        @pl.when((j >= 0) & (j < STEPS) & (y == 0) & (mod(j, 2) == 1))
        def _():
            drain(chunk(up_band, j), right_recv.at[j])

            @pl.when(j >= 7)
            def _():
                drain(chunk(up_band, j - 6), relay_send.at[j - 6])

            send(up_band, j, down_band, relay_send.at[j], relay_recv.at[j])

        @pl.when((j >= 0) & (j < STEPS) & (y > 0))
        def _():
            drain(chunk(down_band, j), left_recv.at[j])

            @pl.when((y == 1) & (j >= BY_ONE))
            def _():
                send(down_band, j, up_band, y_send.at[2], relay_recv.at[j])

            @pl.when((y == 2) & (mod(j, 2) == 0))
            def _():
                @pl.when(j >= 6)
                def _():
                    drain(chunk(down_band, j - 6), relay_send.at[j - 6])

                send(down_band, j, up_band, relay_send.at[j], relay_recv.at[j])

            send(down_band, j, partner, core_send.at[1], core_recv.at[1, div(j, PARTS)])

        return carry

    def take_far(i, carry):
        @pl.when((i >= 0) & (i < STEPS))
        def _():
            drain(chunk(far_band, i), relay_recv.at[i])
            send(far_band, i, partner, core_send.at[3], core_recv.at[3, div(i, PARTS)])

        return carry

    def step(s, carry):
        def due(delay, also=None):
            late = s - delay
            ready = (late >= PARTS - 1) & (late < STEPS - PARTS) & (mod(late, PARTS) == PARTS - 1)
            return (ready if also is None else ready & also), div(late, PARTS)

        other = 1 - 2 * core

        begun = [s >= first for first in WHOLE]
        g1 = sum(one.astype(jnp.int32) for one in begun) - 1
        since = s - WHOLE[0]
        for one, first, last in zip(begun[1:], WHOLE[1:], WHOLE[:-1]):
            since = since - one.astype(jnp.int32) * (first - last)

        @pl.when((since >= 0) & (since < GROUP))
        def _():
            prepare(g1, since)

        @pl.when((since == GROUP) & (g1 < GROUPS - 1))
        def _():
            @pl.when(core == 1)
            def _():
                drain(buf.at[partner, g1], core_recv.at[0, g1])

            gram(g1, y, True)

        ready, g2 = due(LAG + 1, y > 0)

        @pl.when(ready)
        def _():
            drain(buf.at[down_band + other, g2], core_recv.at[1, g2])
            gram(g2, down, False)

        ready, g3 = due(LAG + 3, y == 3)

        @pl.when(ready)
        def _():
            drain(buf.at[up_band + other, g3], core_recv.at[2, g3])
            gram(g3, up, False)

        g4 = (s >= due_far[1]).astype(jnp.int32) + (s >= due_far[2]).astype(jnp.int32)

        @pl.when((y >= 2) & ((s == due_far[0]) | (s == due_far[1]) | (s == due_far[2])))
        def _():
            drain(buf.at[far_band + other, g4], core_recv.at[3, g4])
            gram(g4, far, False)

        begin, end = s + div(s - 1, 4), s + div(s, 4) + 1
        lax.fori_loop(begin, end, front, 0)

        @pl.when(s < 2)
        def _():
            turn(s + 2)
            scatter_all(4 + 2 * s, 6 + 4 * s)

        @pl.when((s < STEPS) & (mod(y, 2) == 0))
        def _():
            @pl.when((s >= FLIGHT) & (s < FEW))
            def _():
                drain(chunk(band, s - FLIGHT), own_send.at[s - FLIGHT])

            @pl.when(s == FEW)
            def _():
                for last in range(FEW - FLIGHT, FEW - 2):
                    drain(chunk(band, last), own_send.at[last])

            @pl.when(s >= FEW)
            def _():
                drain(chunk(band, s - 2), own_send.at[s - 2])

            @pl.when(y == 2)
            def _():
                send(band, s, up_band, own_send.at[s], left_recv.at[s])

            @pl.when(y == 0)
            def _():
                send(band, s, down_band, own_send.at[s], right_recv.at[s])

        @pl.when(y < 3)
        def _():
            lax.fori_loop(begin - LAG, end - LAG, pass_on, 0)

        j = s - LAG

        @pl.when((j >= 0) & (j < STEPS) & (y == 3))
        def _():
            drain(chunk(up_band, j), right_recv.at[j])

            @pl.when(j < BY_ONE)
            def _():
                send(up_band, j, down_band, y_send.at[2], relay_recv.at[j])

            send(up_band, j, partner, core_send.at[2], core_recv.at[2, div(j, PARTS)])
            drain(chunk(down_band, j), left_recv.at[j])
            send(down_band, j, partner, core_send.at[1], core_recv.at[1, div(j, PARTS)])

        @pl.when(y >= 2)
        def _():
            lax.fori_loop(begin - relay, end - relay, take_far, 0)

        for q in range(1, YS):

            @pl.when((s < EARLY) & (y < q))
            def _():
                out_ref[s, :, :, q * WIDE : (q + 1) * WIDE] = jnp.zeros((2, ROWS, WIDE), out_ref.dtype)

        return carry

    lax.fori_loop(0, STEPS + LAG + 1, step, 0)

    other = 1 - 2 * core
    late = GROUPS - 1

    @pl.when(core == 1)
    def _():
        drain(buf.at[partner, late], core_recv.at[0, late])

    for kind, of_band, wanted in ((1, down_band, y > 0), (2, up_band, y == 3), (3, far_band, y >= 2)):

        @pl.when(wanted)
        def _():
            drain(buf.at[of_band + other, late], core_recv.at[kind, late])

    whole = buf.at[band]
    drain(buf.at[band, :, pl.ds(0, CHANS - 1)], a2a_send)

    @pl.when(core == 0)
    def _():
        drain(whole, core_send.at[0])

    @pl.when(y < 2)
    def _():
        drain(whole, y_send.at[0])

    @pl.when(y == 1)
    def _():
        drain(xs.at[pl.ds(0, STEPS - BY_ONE)], y_send.at[2])
        drain(xs.at[pl.ds(0, STEPS // 2)], y_send.at[1])

    @pl.when(mod(y, 2) == 0)
    def _():
        for last in range(STEPS - 2, STEPS):
            drain(chunk(band, last), own_send.at[last])
        for last in (STEPS - 5, STEPS - 3, STEPS - 1):
            drain(chunk(band, 0), relay_send.at[last - div(y, 2)])

    @pl.when(y > 0)
    def _():
        drain(whole, core_send.at[1])

    @pl.when(y == 3)
    def _():
        drain(xs.at[pl.ds(0, BY_ONE)], y_send.at[2])
        drain(whole, core_send.at[2])

    @pl.when(y >= 2)
    def _():
        drain(whole, core_send.at[3])


def correlate(counts, exponents, spectra):
    dma = pltpu.SemaphoreType.DMA
    outs = (
        ((EARLY, 2, ROWS, BANDS * ROWS), jnp.bfloat16),
        ((BANDS, GROUPS, CHANS, GROUP, UNIT, ROWS), jnp.bfloat16),
        ((2, GROUP, 2 * ROWS, DEPTH), jnp.bfloat16),
        ((GROUP, 8, WIDE), jnp.float32),
    )
    return pl.pallas_call(
        kernel,
        out_shape=[pltpu.VMEM(*out) for out in outs],
        in_specs=[pl.BlockSpec(memory_space=pltpu.HBM)] * 3,
        out_specs=[pl.BlockSpec(memory_space=pltpu.VMEM)] * 4,
        scratch_shapes=[
            pltpu.SMEM((OWN,), jnp.int32),
            pltpu.VMEM((CHANS, UNIT, ROWS), jnp.int32),
            pltpu.VMEM((ROWS, CHANS * OWN), jnp.int32),
            pltpu.VMEM((SPANS, 2, ROWS * SAMPLES, LANES), jnp.bfloat16),
            pltpu.VMEM((2, ROWS * SAMPLES, LANES), jnp.float32),
            pltpu.VMEM((LANES * UNIT, ROWS), jnp.float32),
            pltpu.VMEM((CHANS, GROUPS, GROUP, UNIT, ROWS), jnp.bfloat16),
            dma((SPANS + 2,)),
            dma((STEPS,)), dma((STEPS,)), dma((STEPS,)), dma((STEPS,)), dma((4, GROUPS)),
            dma, dma((3,)), dma((STEPS,)), dma((STEPS,)), dma((4,)),
        ],
        compiler_params=pltpu.CompilerParams(
            collective_id=0, has_side_effects=True, vmem_limit_bytes=12 << 20
        ),
        name="correlate",
    )(*(pltpu.with_memory_space_constraint(operand, pltpu.HBM) for operand in (counts, exponents, spectra)))


def finish_kernel(early_ref, buf, forms, shares, out_ref, stage, early_sem, late_sem):
    band = lax.axis_index("band")
    copies = []
    for n in range(OUT_PARTS):
        part = pl.ds(n * (EARLY // OUT_PARTS), EARLY // OUT_PARTS)
        copies.append(pltpu.make_async_copy(early_ref.at[part], out_ref.at[part], early_sem.at[n]))
    for copy in copies:
        copy.start()
    late = GROUPS - 1
    for c in range(GROUP):
        for q in range(YS):
            columns = pl.ds(q * WIDE, WIDE)
            right = jnp.concatenate(
                [buf[2 * q, late, :, c].reshape(DEPTH, ROWS), buf[2 * q + 1, late, :, c].reshape(DEPTH, ROWS)], axis=1
            )
            product = jnp.dot(forms[late % 2, c], right, preferred_element_type=jnp.float32) * shares[c, :1]
            for part in range(2):
                tile = lower(product[part * ROWS : (part + 1) * ROWS], band * ROWS - q * WIDE)
                stage[c, part, :, columns] = tile.astype(jnp.bfloat16)

        copies.append(pltpu.make_async_copy(stage.at[c], out_ref.at[EARLY + c], late_sem.at[c]))
        copies[-1].start()
    for copy in copies:
        copy.wait()


def finish(early, buf, forms, shares):
    vmem = pl.BlockSpec(memory_space=pltpu.VMEM)
    return pl.pallas_call(
        finish_kernel,
        out_shape=jax.ShapeDtypeStruct((OWN, 2, ROWS, BANDS * ROWS), jnp.bfloat16),
        in_specs=[vmem] * 4,
        out_specs=pl.BlockSpec(memory_space=pl.ANY),
        scratch_shapes=[
            pltpu.VMEM((GROUP, 2, ROWS, BANDS * ROWS), jnp.bfloat16),
            pltpu.SemaphoreType.DMA((OUT_PARTS,)),
            pltpu.SemaphoreType.DMA((GROUP,)),
        ],
        compiler_params=pltpu.CompilerParams(vmem_limit_bytes=12 << 20),
        name="finish",
    )(*(pltpu.with_memory_space_constraint(operand, pltpu.VMEM) for operand in (early, buf, forms, shares)))


def local(spectra, exponents, counts):
    flat = jnp.transpose(spectra, (0, 1, 3, 2)).reshape(2, ROWS * SAMPLES, CHANS * OWN)
    return finish(*correlate(counts, exponents, flat))


def solution(mesh):
    placed = (P(None, "band", None, "chan"), P("band", None), P("chan"))
    return jax.shard_map(
        local, mesh=mesh, in_specs=placed, out_specs=P("chan", None, "band", None), check_vma=False
    )
```

time: 215 us -> 94.7 us (0.44)
  waiting for transfers between devices: 136 us -> 0 us
  Pallas kernels: 0 us -> 94.6 us
  other arithmetic: 30.8 us -> 0 us
  matrix products: 17.3 us -> 0 us
  between operations: 13.5 us -> 0.01 us
  starting transfers between devices: 11.1 us -> 0 us
  local copies, waits for them, and re-layouts: 4.23 us -> 0 us
    pallas_call x0 -> x2, Pallas kernels: none -> 94.6 us  [the longest x1 90.9 us: correlate(): pl.pallas_call(kernel, out_shape=[pltpu.VMEM(*out) for out in outs], in_s...]
    all_gather x1 -> x0, waiting for transfers between devices: 87.7 us -> none  [local(): piece = lax.all_gather(plain, 'band', axis=1, tiled=True)]
    all_to_all x1 -> x0, waiting for transfers between devices: 48.3 us -> none  [local(): lax.all_to_all(scaled, 'chan', split_axis=2, concat_axis=3, tiled=True)]
    dot_general x1 -> x0, matrix products: 17.3 us -> none  [gram_tile(): jnp.einsum('crt,cjt->crj', row_form, piece, preferred_element_type=jnp.fl...]
    mul x1 -> x0, other arithmetic: 12.2 us -> none  [compute(): return gram_tile(row_form, piece) * lower_mask(row_start, band_rows, count)]
    convert_element_type x4 -> x0, other arithmetic: 11.6 us -> none  [the longest x1 9.72 us: local(): (tile / counts.astype(jnp.float32)[:, None, None, None]).astype(jnp.bfloa...]
    all_to_all x1 -> x0, starting transfers between devices: 11 us -> none  [local(): lax.all_to_all(scaled, 'chan', split_axis=2, concat_axis=3, tiled=True)]
    concatenate x1 -> x0, other arithmetic: 4.18 us -> none  [forms(): return (plain, jnp.concatenate([plain, rotated], axis=1))]
  transfers between devices with their start and end apart: 2 -> 0, of which waited for: 2 -> 0; matrix products, arithmetic and copies ran while one was open for 2% -> 0% of each run, Pallas kernels for 0% -> 0%
where the time goes in v1:
time: 94.7 us; the launch traced here: 94.6 us
  Pallas kernels  94.6 us (100%)
    pallas_call x1, Pallas kernels, correlate(): pl.pallas_call(kernel, out_shape=[pltpu.VMEM(*out) for out in outs], in_s...  90.9 us
    pallas_call x1, Pallas kernels, finish(): pl.pallas_call(finish_kernel, out_shape=jax.ShapeDtypeStruct((OWN, 2, ROW...  3.71 us

profile of v1, /device:TPU:25, one launch (start us, length us, event | category | flops | bytes accessed | tf_op | source)
XLA Modules:
  0.0 94.6 jit_solution(12251531245955233008)
XLA Ops:
  0.0 90.9 %correlate.1 = (bf16[12,2,128,1024]{3,2,1,0:T(8,128)(2,1)S(1)}, bf16[8,4,32,4,16,128]{5,4,3,2,1,0:T(8,128)(2,1)S(1)}, bf16[2,4,256,512]{3,2,1,0:T(8,128)(2,1)S(1)}, f32[4,8,256]{2,1,0:T(8,128)S(1)}) custom-call(s32[16]{0:T(128)} %counts_hbm.1, s32[128,512]{1,0:T(8,128)} %exponents_ref.1, bf16[2,1024,512]{2,1,0:T(8,128)(2,1)} %bitcast.3), custom_call_target="tpu_custom_call" | custom-call | tf_op jit(solution)/shard_map/correlate/pallas_call | solution.py:443
  90.9 3.7 %finish.1 = bf16[16,2,128,1024]{3,2,1,0:T(8,128)(2,1)} custom-call(bf16[12,2,128,1024]{3,2,1,0:T(8,128)(2,1)S(1)} %get-tuple-element.9.early_ref, bf16[8,4,32,4,16,128]{5,4,3,2,1,0:T(8,128)(2,1)S(1)} %get-tuple-element.10.buf, bf16[2,4,256,512]{3,2,1,0:T(8,128)(2,1)S(1)} %get-tuple-element.11.forms, f32[4,8,256]{2,1,0:T(8,128)S(1)} %get-tuple-element.12.shares), custom_call_target="tpu_custom_call" | custom-call | tf_op jit(solution)/shard_map/finish/pallas_call | solution.py:495

commit v2 on v1

--- a/solution.py
+++ b/solution.py
@@ -22,13 +22,15 @@
 CHUNK = 4
 PARTS = CHANS // CHUNK
 STEPS = GROUPS * PARTS
-WHOLE = (7, 13, 20, 26)
-AHEAD = 12
+WHOLE = 12, 17, 22, 27
+DIRECT = 17, 23, 29
+SECOND = 19, 25, 31
+AHEAD = 13
 BY_ONE = 24
 LANES = 128
 SPANS = CHANS * OWN // LANES
 LAG = 3
-FIRST = 4
+NEAR = 2 * GROUPS
 FEW = 28
 FLIGHT = 4
 OUT_PARTS = 6
@@ -55,6 +57,13 @@
 
 def offset(k):
     return 2 * div(k, 2 * CHUNK) + mod(k, 2), div(mod(k, CHUNK), 2) + 2 * mod(div(k, CHUNK), 2)
+
+
+def place(s):
+    near = int(s < NEAR) if isinstance(s, int) else (s < NEAR).astype(jnp.int32)
+    rest = s - NEAR
+    group = near * div(s, 2) + (1 - near) * div(rest, PARTS - 2)
+    return group, near * mod(s, 2) + (1 - near) * (2 + mod(rest, PARTS - 2))
 
 
 def source(chan, k):
@@ -85,7 +94,7 @@
     up, down, far = mod(y + 1, YS), mod(y + YS - 1, YS), mod(y + 2, YS)
     slow = (y == 2).astype(jnp.int32)
     relay = 9 + 3 * slow
-    due_far = 14 + 3 * slow, 21 + 2 * slow, 27 + 2 * slow
+    due_far = 20 + slow, 24 + 2 * slow, 30 + slow
     up_band, down_band, far_band = up * CORES + core, down * CORES + core, far * CORES + core
 
     barrier = pltpu.get_barrier_semaphore()
@@ -133,12 +142,12 @@
     loads[0].wait()
     turn(0)
     for g in range(GROUPS):
-        pltpu.make_async_copy(xs.at[chan, g], buf.at[band, g, 0], a2a_recv.at[g * PARTS]).start()
+        pltpu.make_async_copy(xs.at[chan, g], buf.at[band, g, 0], a2a_recv.at[2 * g]).start()
 
     pl.semaphore_wait(barrier, CHANS + 2)
 
     def scatter(s):
-        g, part = div(s, PARTS), mod(s, PARTS)
+        g, part = place(s)
 
         for n in range(CHUNK):
             k = part * CHUNK + n
@@ -159,9 +168,7 @@
 
         lax.fori_loop(first, end, one, 0)
 
-    scatter_all(0, 2)
-    turn(1)
-    scatter_all(2, 4)
+    scatter_all(0, NEAR // 2)
 
     piece = lax.broadcasted_iota(jnp.int32, times.shape, 0)
     row = lax.broadcasted_iota(jnp.int32, times.shape, 1)
@@ -171,7 +178,7 @@
         shares[c] = 1.0 / jnp.full(shares.shape[1:], counts_ref[EARLY + c], jnp.int32).astype(jnp.float32)
 
     def chunk(of_band, s):
-        g, part = div(s, PARTS), mod(s, PARTS)
+        g, part = place(s)
         return buf.at[of_band, g, pl.ds(part * CHUNK, CHUNK)]
 
     def send(of_band, s, to_band, send_sem, recv_sem):
@@ -220,14 +227,9 @@
 
             @pl.when(core == 0)
             def _():
-                send(band, s, partner, core_send.at[0], core_recv.at[0, div(s, PARTS)])
-
-        @pl.when((s > 2) & (s < AHEAD - FIRST))
-        def _():
-            scatter(2 * s + FIRST)
-            scatter(2 * s + FIRST + 1)
-
-        @pl.when((s >= AHEAD - FIRST) & (s + AHEAD < STEPS))
+                send(band, s, partner, core_send.at[0], core_recv.at[0, place(s)[0]])
+
+        @pl.when((s > 2) & (s + AHEAD < STEPS))
         def _():
             scatter(s + AHEAD)
 
@@ -260,7 +262,7 @@
 
                 send(down_band, j, up_band, relay_send.at[j], relay_recv.at[j])
 
-            send(down_band, j, partner, core_send.at[1], core_recv.at[1, div(j, PARTS)])
+            send(down_band, j, partner, core_send.at[1], core_recv.at[1, place(j)[0]])
 
         return carry
 
@@ -268,15 +270,14 @@
         @pl.when((i >= 0) & (i < STEPS))
         def _():
             drain(chunk(far_band, i), relay_recv.at[i])
-            send(far_band, i, partner, core_send.at[3], core_recv.at[3, div(i, PARTS)])
+            send(far_band, i, partner, core_send.at[3], core_recv.at[3, place(i)[0]])
 
         return carry
 
     def step(s, carry):
-        def due(delay, also=None):
-            late = s - delay
-            ready = (late >= PARTS - 1) & (late < STEPS - PARTS) & (mod(late, PARTS) == PARTS - 1)
-            return (ready if also is None else ready & also), div(late, PARTS)
+        def due(steps):
+            ready = (s == steps[0]) | (s == steps[1]) | (s == steps[2])
+            return ready, (s >= steps[1]).astype(jnp.int32) + (s >= steps[2]).astype(jnp.int32)
 
         other = 1 - 2 * core
 
@@ -298,23 +299,23 @@
 
             gram(g1, y, True)
 
-        ready, g2 = due(LAG + 1, y > 0)
-
-        @pl.when(ready)
+        ready, g2 = due(DIRECT)
+
+        @pl.when(ready & (y > 0))
         def _():
             drain(buf.at[down_band + other, g2], core_recv.at[1, g2])
             gram(g2, down, False)
 
-        ready, g3 = due(LAG + 3, y == 3)
-
-        @pl.when(ready)
+        ready, g3 = due(SECOND)
+
+        @pl.when(ready & (y == 3))
         def _():
             drain(buf.at[up_band + other, g3], core_recv.at[2, g3])
             gram(g3, up, False)
 
-        g4 = (s >= due_far[1]).astype(jnp.int32) + (s >= due_far[2]).astype(jnp.int32)
-
-        @pl.when((y >= 2) & ((s == due_far[0]) | (s == due_far[1]) | (s == due_far[2])))
+        ready, g4 = due(due_far)
+
+        @pl.when(ready & (y >= 2))
         def _():
             drain(buf.at[far_band + other, g4], core_recv.at[3, g4])
             gram(g4, far, False)
@@ -322,11 +323,6 @@
         begin, end = s + div(s - 1, 4), s + div(s, 4) + 1
         lax.fori_loop(begin, end, front, 0)
 
-        @pl.when(s < 2)
-        def _():
-            turn(s + 2)
-            scatter_all(4 + 2 * s, 6 + 4 * s)
-
         @pl.when((s < STEPS) & (mod(y, 2) == 0))
         def _():
             @pl.when((s >= FLIGHT) & (s < FEW))
@@ -350,6 +346,19 @@
             def _():
                 send(band, s, down_band, own_send.at[s], right_recv.at[s])
 
+        @pl.when(s == 0)
+        def _():
+            scatter_all(NEAR // 2, NEAR)
+
+        @pl.when(s < SPANS - 1)
+        def _():
+            turn(s + 1)
+            scatter_all(NEAR + 2 * s, NEAR + 2 * s + 2)
+
+        @pl.when(s == SPANS - 2)
+        def _():
+            scatter_all(NEAR + 2 * SPANS - 2, AHEAD + 3)
+
         @pl.when(y < 3)
         def _():
             lax.fori_loop(begin - LAG, end - LAG, pass_on, 0)
@@ -364,9 +373,9 @@
             def _():
                 send(up_band, j, down_band, y_send.at[2], relay_recv.at[j])
 
-            send(up_band, j, partner, core_send.at[2], core_recv.at[2, div(j, PARTS)])
+            send(up_band, j, partner, core_send.at[2], core_recv.at[2, place(j)[0]])
             drain(chunk(down_band, j), left_recv.at[j])
-            send(down_band, j, partner, core_send.at[1], core_recv.at[1, div(j, PARTS)])
+            send(down_band, j, partner, core_send.at[1], core_recv.at[1, place(j)[0]])
 
         @pl.when(y >= 2)
         def _():

time: 94.7 us -> 92.6 us (0.978)
  Pallas kernels: 94.6 us -> 92.5 us
    pallas_call x1, Pallas kernels: 90.9 us -> 88.8 us  [correlate(): pl.pallas_call(kernel, out_shape=[pltpu.VMEM(*out) for out in outs], in_s...]
where the time goes in v2:
time: 92.6 us; the launch traced here: 92.5 us
  Pallas kernels  92.5 us (100%)
    pallas_call x1, Pallas kernels, correlate(): pl.pallas_call(kernel, out_shape=[pltpu.VMEM(*out) for out in outs], in_s...  88.8 us
    pallas_call x1, Pallas kernels, finish(): pl.pallas_call(finish_kernel, out_shape=jax.ShapeDtypeStruct((OWN, 2, ROW...  3.71 us

profile of v2, /device:TPU:25, one launch (start us, length us, event | category | flops | bytes accessed | tf_op | source)
XLA Modules:
  0.0 92.5 jit_solution(17983533358304351359)
XLA Ops:
  0.0 88.8 %correlate.1 = (bf16[12,2,128,1024]{3,2,1,0:T(8,128)(2,1)S(1)}, bf16[8,4,32,4,16,128]{5,4,3,2,1,0:T(8,128)(2,1)S(1)}, bf16[2,4,256,512]{3,2,1,0:T(8,128)(2,1)S(1)}, f32[4,8,256]{2,1,0:T(8,128)S(1)}) custom-call(s32[16]{0:T(128)} %counts_hbm.1, s32[128,512]{1,0:T(8,128)} %exponents_ref.1, bf16[2,1024,512]{2,1,0:T(8,128)(2,1)} %bitcast.3), custom_call_target="tpu_custom_call" | custom-call | tf_op jit(solution)/shard_map/correlate/pallas_call | solution.py:452
  88.8 3.7 %finish.1 = bf16[16,2,128,1024]{3,2,1,0:T(8,128)(2,1)} custom-call(bf16[12,2,128,1024]{3,2,1,0:T(8,128)(2,1)S(1)} %get-tuple-element.9.early_ref, bf16[8,4,32,4,16,128]{5,4,3,2,1,0:T(8,128)(2,1)S(1)} %get-tuple-element.10.buf, bf16[2,4,256,512]{3,2,1,0:T(8,128)(2,1)S(1)} %get-tuple-element.11.forms, f32[4,8,256]{2,1,0:T(8,128)S(1)} %get-tuple-element.12.shares), custom_call_target="tpu_custom_call" | custom-call | tf_op jit(solution)/shard_map/finish/pallas_call | solution.py:504

commit v3 on v2

--- a/solution.py
+++ b/solution.py
@@ -25,7 +25,7 @@
 WHOLE = 12, 17, 22, 27
 DIRECT = 17, 23, 29
 SECOND = 19, 25, 31
-AHEAD = 13
+AHEAD = 16
 BY_ONE = 24
 LANES = 128
 SPANS = CHANS * OWN // LANES
@@ -325,18 +325,15 @@
 
         @pl.when((s < STEPS) & (mod(y, 2) == 0))
         def _():
-            @pl.when((s >= FLIGHT) & (s < FEW))
-            def _():
-                drain(chunk(band, s - FLIGHT), own_send.at[s - FLIGHT])
-
-            @pl.when(s == FEW)
-            def _():
-                for last in range(FEW - FLIGHT, FEW - 2):
-                    drain(chunk(band, last), own_send.at[last])
+            flight = FLIGHT - core
+
+            @pl.when((s >= flight) & (s <= FEW))
+            def _():
+                drain(chunk(band, s - flight), own_send.at[s - flight])
 
             @pl.when(s >= FEW)
             def _():
-                drain(chunk(band, s - 2), own_send.at[s - 2])
+                drain(chunk(band, s - flight + 1), own_send.at[s - flight + 1])
 
             @pl.when(y == 2)
             def _():
@@ -422,8 +419,13 @@
 
     @pl.when(mod(y, 2) == 0)
     def _():
+        @pl.when(core == 0)
+        def _():
+            drain(chunk(band, STEPS - 3), own_send.at[STEPS - 3])
+
         for last in range(STEPS - 2, STEPS):
             drain(chunk(band, last), own_send.at[last])
+
         for last in (STEPS - 5, STEPS - 3, STEPS - 1):
             drain(chunk(band, 0), relay_send.at[last - div(y, 2)])
 

time: 92.6 us -> 92.2 us (level)
  no operation moved by 1% of the time
where the time goes in v3:
time: 92.2 us; the launch traced here: 92.1 us
  Pallas kernels  92.1 us (100%)
    pallas_call x1, Pallas kernels, correlate(): pl.pallas_call(kernel, out_shape=[pltpu.VMEM(*out) for out in outs], in_s...  88.4 us
    pallas_call x1, Pallas kernels, finish(): pl.pallas_call(finish_kernel, out_shape=jax.ShapeDtypeStruct((OWN, 2, ROW...  3.72 us

profile of v3, /device:TPU:25, one launch (start us, length us, event | category | flops | bytes accessed | tf_op | source)
XLA Modules:
  0.0 92.1 jit_solution(16981502681558531355)
XLA Ops:
  0.0 88.4 %correlate.1 = (bf16[12,2,128,1024]{3,2,1,0:T(8,128)(2,1)S(1)}, bf16[8,4,32,4,16,128]{5,4,3,2,1,0:T(8,128)(2,1)S(1)}, bf16[2,4,256,512]{3,2,1,0:T(8,128)(2,1)S(1)}, f32[4,8,256]{2,1,0:T(8,128)S(1)}) custom-call(s32[16]{0:T(128)} %counts_hbm.1, s32[128,512]{1,0:T(8,128)} %exponents_ref.1, bf16[2,1024,512]{2,1,0:T(8,128)(2,1)} %bitcast.3), custom_call_target="tpu_custom_call" | custom-call | tf_op jit(solution)/shard_map/correlate/pallas_call | solution.py:454
  88.4 3.7 %finish.1 = bf16[16,2,128,1024]{3,2,1,0:T(8,128)(2,1)} custom-call(bf16[12,2,128,1024]{3,2,1,0:T(8,128)(2,1)S(1)} %get-tuple-element.9.early_ref, bf16[8,4,32,4,16,128]{5,4,3,2,1,0:T(8,128)(2,1)S(1)} %get-tuple-element.10.buf, bf16[2,4,256,512]{3,2,1,0:T(8,128)(2,1)S(1)} %get-tuple-element.11.forms, f32[4,8,256]{2,1,0:T(8,128)S(1)} %get-tuple-element.12.shares), custom_call_target="tpu_custom_call" | custom-call | tf_op jit(solution)/shard_map/finish/pallas_call | solution.py:506

commit v4 on v3

--- a/solution.py
+++ b/solution.py
@@ -225,7 +225,7 @@
             def _():
                 send(band, s, down_band, y_send.at[1], right_recv.at[s])
 
-            @pl.when(core == 0)
+            @pl.when((core == 0) & ((mod(y, 2) == 1) | (place(s)[0] < GROUPS - 1)))
             def _():
                 send(band, s, partner, core_send.at[0], core_recv.at[0, place(s)[0]])
 
@@ -270,7 +270,10 @@
         @pl.when((i >= 0) & (i < STEPS))
         def _():
             drain(chunk(far_band, i), relay_recv.at[i])
-            send(far_band, i, partner, core_send.at[3], core_recv.at[3, place(i)[0]])
+
+            @pl.when((y == 3) | (place(i)[0] < GROUPS - 1))
+            def _():
+                send(far_band, i, partner, core_send.at[3], core_recv.at[3, place(i)[0]])
 
         return carry
 
@@ -391,6 +394,33 @@
     other = 1 - 2 * core
     late = GROUPS - 1
 
+    @pl.when(mod(y, 2) == 0)
+    def _():
+        @pl.when(core == 0)
+        def _():
+            drain(chunk(band, STEPS - 3), own_send.at[STEPS - 3])
+
+        for last in range(STEPS - 2, STEPS):
+            drain(chunk(band, last), own_send.at[last])
+
+        for last in (STEPS - 5, STEPS - 3, STEPS - 1):
+            drain(chunk(band, 0), relay_send.at[last - div(y, 2)])
+
+    def send_late(of_band, send_sem, recv_sem):
+        ref = buf.at[of_band, late]
+        pltpu.make_async_remote_copy(
+            src_ref=ref, dst_ref=ref, send_sem=send_sem, recv_sem=recv_sem,
+            device_id=(partner, chan), device_id_type=MESH,
+        ).start()
+
+    @pl.when((core == 0) & (mod(y, 2) == 0))
+    def _():
+        send_late(band, core_send.at[0], core_recv.at[0, late])
+
+    @pl.when(y == 2)
+    def _():
+        send_late(far_band, core_send.at[3], core_recv.at[3, late])
+
     @pl.when(core == 1)
     def _():
         drain(buf.at[partner, late], core_recv.at[0, late])
@@ -416,18 +446,6 @@
     def _():
         drain(xs.at[pl.ds(0, STEPS - BY_ONE)], y_send.at[2])
         drain(xs.at[pl.ds(0, STEPS // 2)], y_send.at[1])
-
-    @pl.when(mod(y, 2) == 0)
-    def _():
-        @pl.when(core == 0)
-        def _():
-            drain(chunk(band, STEPS - 3), own_send.at[STEPS - 3])
-
-        for last in range(STEPS - 2, STEPS):
-            drain(chunk(band, last), own_send.at[last])
-
-        for last in (STEPS - 5, STEPS - 3, STEPS - 1):
-            drain(chunk(band, 0), relay_send.at[last - div(y, 2)])
 
     @pl.when(y > 0)
     def _():

time: 92.2 us -> 92.9 us (level)
  no operation moved by 1% of the time
where the time goes in v4:
time: 92.9 us; the launch traced here: 92.1 us
  Pallas kernels  92.1 us (99%)
    pallas_call x1, Pallas kernels, correlate(): pl.pallas_call(kernel, out_shape=[pltpu.VMEM(*out) for out in outs], in_s...  88.4 us
    pallas_call x1, Pallas kernels, finish(): pl.pallas_call(finish_kernel, out_shape=jax.ShapeDtypeStruct((OWN, 2, ROW...  3.72 us

profile of v4, /device:TPU:25, one launch (start us, length us, event | category | flops | bytes accessed | tf_op | source)
XLA Modules:
  0.0 92.1 jit_solution(8680754163863106546)
XLA Ops:
  0.0 88.4 %correlate.1 = (bf16[12,2,128,1024]{3,2,1,0:T(8,128)(2,1)S(1)}, bf16[8,4,32,4,16,128]{5,4,3,2,1,0:T(8,128)(2,1)S(1)}, bf16[2,4,256,512]{3,2,1,0:T(8,128)(2,1)S(1)}, f32[4,8,256]{2,1,0:T(8,128)S(1)}) custom-call(s32[16]{0:T(128)} %counts_hbm.1, s32[128,512]{1,0:T(8,128)} %exponents_ref.1, bf16[2,1024,512]{2,1,0:T(8,128)(2,1)} %bitcast.3), custom_call_target="tpu_custom_call" | custom-call | tf_op jit(solution)/shard_map/correlate/pallas_call | solution.py:472
  88.4 3.7 %finish.1 = bf16[16,2,128,1024]{3,2,1,0:T(8,128)(2,1)} custom-call(bf16[12,2,128,1024]{3,2,1,0:T(8,128)(2,1)S(1)} %get-tuple-element.9.early_ref, bf16[8,4,32,4,16,128]{5,4,3,2,1,0:T(8,128)(2,1)S(1)} %get-tuple-element.10.buf, bf16[2,4,256,512]{3,2,1,0:T(8,128)(2,1)S(1)} %get-tuple-element.11.forms, f32[4,8,256]{2,1,0:T(8,128)S(1)} %get-tuple-element.12.shares), custom_call_target="tpu_custom_call" | custom-call | tf_op jit(solution)/shard_map/finish/pallas_call | solution.py:524

commit v5 on v3

--- a/solution.py
+++ b/solution.py
@@ -22,7 +22,7 @@
 CHUNK = 4
 PARTS = CHANS // CHUNK
 STEPS = GROUPS * PARTS
-WHOLE = 12, 17, 22, 27
+WHOLE = 12, 17, 22, 26
 DIRECT = 17, 23, 29
 SECOND = 19, 25, 31
 AHEAD = 16
@@ -130,7 +130,7 @@
             wide[part] = raw[n, part].astype(jnp.float32)
             for t in range(SAMPLES):
                 tile = wide[part, pl.ds(t, ROWS, stride=SAMPLES), :] * scale
-                narrow[pl.ds(part * SAMPLES + t, LANES, stride=UNIT), :] = tile.T
+                narrow[pl.ds(part * SAMPLES + t, LANES, stride=UNIT), :] = tile.astype(jnp.bfloat16).T.astype(jnp.float32)
 
         def pack(d, carry):
             own = narrow[pl.ds(pl.multiple_of(d * (OWN * UNIT), OWN * UNIT), OWN * UNIT), :]
@@ -281,6 +281,27 @@
 
         other = 1 - 2 * core
 
+        ready, g2 = due(DIRECT)
+
+        @pl.when(ready & (y > 0))
+        def _():
+            drain(buf.at[down_band + other, g2], core_recv.at[1, g2])
+            gram(g2, down, False)
+
+        ready, g3 = due(SECOND)
+
+        @pl.when(ready & (y == 3))
+        def _():
+            drain(buf.at[up_band + other, g3], core_recv.at[2, g3])
+            gram(g3, up, False)
+
+        ready, g4 = due(due_far)
+
+        @pl.when(ready & (y >= 2))
+        def _():
+            drain(buf.at[far_band + other, g4], core_recv.at[3, g4])
+            gram(g4, far, False)
+
         begun = [s >= first for first in WHOLE]
         g1 = sum(one.astype(jnp.int32) for one in begun) - 1
         since = s - WHOLE[0]
@@ -291,34 +312,13 @@
         def _():
             prepare(g1, since)
 
-        @pl.when((since == GROUP) & (g1 < GROUPS - 1))
+        @pl.when((since == GROUP - 1) & (g1 < GROUPS - 1))
         def _():
             @pl.when(core == 1)
             def _():
                 drain(buf.at[partner, g1], core_recv.at[0, g1])
 
             gram(g1, y, True)
-
-        ready, g2 = due(DIRECT)
-
-        @pl.when(ready & (y > 0))
-        def _():
-            drain(buf.at[down_band + other, g2], core_recv.at[1, g2])
-            gram(g2, down, False)
-
-        ready, g3 = due(SECOND)
-
-        @pl.when(ready & (y == 3))
-        def _():
-            drain(buf.at[up_band + other, g3], core_recv.at[2, g3])
-            gram(g3, up, False)
-
-        ready, g4 = due(due_far)
-
-        @pl.when(ready & (y >= 2))
-        def _():
-            drain(buf.at[far_band + other, g4], core_recv.at[3, g4])
-            gram(g4, far, False)
 
         begin, end = s + div(s - 1, 4), s + div(s, 4) + 1
         lax.fori_loop(begin, end, front, 0)

time: 92.2 us -> 92.3 us (level)
  no operation moved by 1% of the time
where the time goes in v5:
time: 92.3 us; the launch traced here: 92.2 us
  Pallas kernels  92.2 us (100%)
    pallas_call x1, Pallas kernels, correlate(): pl.pallas_call(kernel, out_shape=[pltpu.VMEM(*out) for out in outs], in_s...  88.5 us
    pallas_call x1, Pallas kernels, finish(): pl.pallas_call(finish_kernel, out_shape=jax.ShapeDtypeStruct((OWN, 2, ROW...  3.72 us

profile of v5, /device:TPU:25, one launch (start us, length us, event | category | flops | bytes accessed | tf_op | source)
XLA Modules:
  0.0 92.2 jit_solution(6042683733993858183)
XLA Ops:
  0.0 88.5 %correlate.1 = (bf16[12,2,128,1024]{3,2,1,0:T(8,128)(2,1)S(1)}, bf16[8,4,32,4,16,128]{5,4,3,2,1,0:T(8,128)(2,1)S(1)}, bf16[2,4,256,512]{3,2,1,0:T(8,128)(2,1)S(1)}, f32[4,8,256]{2,1,0:T(8,128)S(1)}) custom-call(s32[16]{0:T(128)} %counts_hbm.1, s32[128,512]{1,0:T(8,128)} %exponents_ref.1, bf16[2,1024,512]{2,1,0:T(8,128)(2,1)} %bitcast.3), custom_call_target="tpu_custom_call" | custom-call | tf_op jit(solution)/shard_map/correlate/pallas_call | solution.py:454
  88.5 3.7 %finish.1 = bf16[16,2,128,1024]{3,2,1,0:T(8,128)(2,1)} custom-call(bf16[12,2,128,1024]{3,2,1,0:T(8,128)(2,1)S(1)} %get-tuple-element.9.early_ref, bf16[8,4,32,4,16,128]{5,4,3,2,1,0:T(8,128)(2,1)S(1)} %get-tuple-element.10.buf, bf16[2,4,256,512]{3,2,1,0:T(8,128)(2,1)S(1)} %get-tuple-element.11.forms, f32[4,8,256]{2,1,0:T(8,128)S(1)} %get-tuple-element.12.shares), custom_call_target="tpu_custom_call" | custom-call | tf_op jit(solution)/shard_map/finish/pallas_call | solution.py:506

commit v6 on v3

--- a/solution.py
+++ b/solution.py
@@ -55,8 +55,12 @@
     return sum(mod(div(a, 1 << n) + div(b, 1 << n), 2) * (1 << n) for n in range(bits))
 
 
+def far_first(n):
+    return 2 * mod(n, 2) + div(n, 2)
+
+
 def offset(k):
-    return 2 * div(k, 2 * CHUNK) + mod(k, 2), div(mod(k, CHUNK), 2) + 2 * mod(div(k, CHUNK), 2)
+    return 2 * far_first(div(k, 2 * CHUNK)) + mod(k, 2), div(mod(k, CHUNK), 2) + 2 * mod(div(k, CHUNK), 2)
 
 
 def place(s):
@@ -107,7 +111,7 @@
         pltpu.make_async_copy(ref, ref, sem).wait()
 
     def span(n):
-        return flip(div(chan, 2 * XS), n, 2)
+        return flip(div(chan, 2 * XS), far_first(n), 2)
 
     def lanes(n):
         return pl.ds(pl.multiple_of(span(n) * LANES, LANES), LANES)
@@ -169,6 +173,8 @@
         lax.fori_loop(first, end, one, 0)
 
     scatter_all(0, NEAR // 2)
+    turn(1)
+    scatter_all(NEAR, NEAR + 2)
 
     piece = lax.broadcasted_iota(jnp.int32, times.shape, 0)
     row = lax.broadcasted_iota(jnp.int32, times.shape, 1)
@@ -347,12 +353,12 @@
         def _():
             scatter_all(NEAR // 2, NEAR)
 
-        @pl.when(s < SPANS - 1)
-        def _():
-            turn(s + 1)
-            scatter_all(NEAR + 2 * s, NEAR + 2 * s + 2)
-
-        @pl.when(s == SPANS - 2)
+        @pl.when(s < SPANS - 2)
+        def _():
+            turn(s + 2)
+            scatter_all(NEAR + 2 * s + 2, NEAR + 2 * s + 4)
+
+        @pl.when(s == SPANS - 3)
         def _():
             scatter_all(NEAR + 2 * SPANS - 2, AHEAD + 3)
 

time: 92.2 us -> 91 us (0.987)
  Pallas kernels: 92.1 us -> 90.9 us
    pallas_call x1, Pallas kernels: 88.4 us -> 87.2 us  [correlate(): pl.pallas_call(kernel, out_shape=[pltpu.VMEM(*out) for out in outs], in_s...]
where the time goes in v6:
time: 91 us
  Pallas kernels  90.9 us (100%)
    pallas_call x1, Pallas kernels, correlate(): pl.pallas_call(kernel, out_shape=[pltpu.VMEM(*out) for out in outs], in_s...  87.2 us
    pallas_call x1, Pallas kernels, finish(): pl.pallas_call(finish_kernel, out_shape=jax.ShapeDtypeStruct((OWN, 2, ROW...  3.71 us

profile of v6, /device:TPU:25, one launch (start us, length us, event | category | flops | bytes accessed | tf_op | source)
XLA Modules:
  0.0 91.0 jit_solution(9403979345728560842)
XLA Ops:
  0.0 87.2 %correlate.1 = (bf16[12,2,128,1024]{3,2,1,0:T(8,128)(2,1)S(1)}, bf16[8,4,32,4,16,128]{5,4,3,2,1,0:T(8,128)(2,1)S(1)}, bf16[2,4,256,512]{3,2,1,0:T(8,128)(2,1)S(1)}, f32[4,8,256]{2,1,0:T(8,128)S(1)}) custom-call(s32[16]{0:T(128)} %counts_hbm.1, s32[128,512]{1,0:T(8,128)} %exponents_ref.1, bf16[2,1024,512]{2,1,0:T(8,128)(2,1)} %bitcast.3), custom_call_target="tpu_custom_call" | custom-call | tf_op jit(solution)/shard_map/correlate/pallas_call | solution.py:460
  87.2 3.7 %finish.1 = bf16[16,2,128,1024]{3,2,1,0:T(8,128)(2,1)} custom-call(bf16[12,2,128,1024]{3,2,1,0:T(8,128)(2,1)S(1)} %get-tuple-element.9.early_ref, bf16[8,4,32,4,16,128]{5,4,3,2,1,0:T(8,128)(2,1)S(1)} %get-tuple-element.10.buf, bf16[2,4,256,512]{3,2,1,0:T(8,128)(2,1)S(1)} %get-tuple-element.11.forms, f32[4,8,256]{2,1,0:T(8,128)S(1)} %get-tuple-element.12.shares), custom_call_target="tpu_custom_call" | custom-call | tf_op jit(solution)/shard_map/finish/pallas_call | solution.py:512
